TPU v7x, 128 devices: a whole 4x4x4 slice. The times are simulated.
128 devices in a mesh: dp: 8 (over x, core), ctx: 16 (over y, z).
Axes of the slice: x: 4, y: 4, z: 4, core: 2. Of those that a mesh axis runs over, the one named last changes fastest.
Arguments:
- query_matrix: bfloat16 [16384, 4096], P(('dp', 'ctx')), may hold values from -162 to 162
- key_matrix: bfloat16 [16384, 512], P(('dp', 'ctx')), may hold values from -6 to 6
- value_matrix: bfloat16 [16384, 512], P(('dp', 'ctx')), may hold values from -6 to 6
- output_gradient: bfloat16 [16384, 4096], P(('dp', 'ctx')), may hold values from -6 to 6
- document_length_list: int32 [96], replicated, may hold values from 1 to 256, 16384 in all
- slab_plan: int32 [8, 16, 16], P('dp'), may hold values from 0 to 15, as said below
Outputs:
- attended: bfloat16 [16384, 4096], P(('dp', 'ctx'))
- query_grads: bfloat16 [16384, 4096], P(('dp', 'ctx'))
- key_grads: bfloat16 [16384, 512], P(('dp', 'ctx'))
- value_grads: bfloat16 [16384, 512], P(('dp', 'ctx'))
Inputs may be any that keep to these rules, and one draw needn't show every extreme that they name: `document_length_list`: the lengths add up to 16384 and the longest is exactly 256. For every g and o, slab_plan[g, o, :] names each of 0 to 15 once.
All inputs are finite; a program needn't handle non-finite values.
Results may differ from a plain program's by a relative error of at most 0.04.
Values may be sent and summed in bfloat16 or wider, within the bound.
A program may use at most 128 MiB of HBM per device.

v0:
```python
from functools import partial
import math

import jax
import jax.numpy as jnp
from jax import lax
from jax.sharding import PartitionSpec as P

KEY_VALUE_HEADS = 4
HEAD_WIDTH = 128


def shifted(x, axis, by):
    size = lax.axis_size(axis)
    pairs = [(i, i + by) for i in range(size) if 0 <= i + by < size]
    return lax.ppermute(x, axis, pairs)


def doc_first(positions, document_length_list):
    doc_ends = jnp.cumsum(document_length_list)
    ended = doc_ends[None, :] <= positions[:, None]
    return jnp.sum(jnp.where(ended, document_length_list[None, :], 0), axis=1)


def attend_over_span(
    rows_q, rows_d, q_pos, rows_k, rows_v, k_pos, document_length_list, key_value_count
):
    heads_per_group = rows_q.shape[1] // (key_value_count * HEAD_WIDTH)
    scale = 1.0 / math.sqrt(HEAD_WIDTH)
    first_pos = doc_first(q_pos, document_length_list)
    visible = (k_pos[None, :] >= first_pos[:, None]) & (k_pos[None, :] <= q_pos[:, None])
    row_count = rows_q.shape[0]
    out_parts = []
    dq_parts = []
    key_terms = []
    value_terms = []
    for kv_head in range(key_value_count):
        col_low = kv_head * heads_per_group * HEAD_WIDTH
        col_high = col_low + heads_per_group * HEAD_WIDTH
        query_block_tile = rows_q[:, col_low:col_high].reshape(
            row_count, heads_per_group, HEAD_WIDTH
        )
        delta_block = rows_d[:, col_low:col_high].reshape(row_count, heads_per_group, HEAD_WIDTH)
        key_block_tile = rows_k[:, kv_head * HEAD_WIDTH : (kv_head + 1) * HEAD_WIDTH]
        value_block_tile = rows_v[:, kv_head * HEAD_WIDTH : (kv_head + 1) * HEAD_WIDTH]
        scores = (
            jnp.einsum(
                "igd,jd->gij", query_block_tile, key_block_tile, preferred_element_type=jnp.float32
            )
            * scale
        )
        scores = jnp.where(visible[None], scores, jnp.float32(-1e30))
        row_max = jnp.max(scores, axis=-1, keepdims=True)
        log_sum = row_max + jnp.log(jnp.sum(jnp.exp(scores - row_max), axis=-1, keepdims=True))
        probs = jnp.exp(scores - log_sum)
        probability_block = probs.astype(jnp.bfloat16)
        out_b = jnp.einsum(
            "gij,jd->igd", probability_block, value_block_tile, preferred_element_type=jnp.float32
        ).astype(jnp.bfloat16)
        delta = jnp.transpose(
            jnp.sum(delta_block.astype(jnp.float32) * out_b.astype(jnp.float32), axis=-1), (1, 0)
        )
        d_probs = jnp.einsum(
            "igd,jd->gij", delta_block, value_block_tile, preferred_element_type=jnp.float32
        )
        scores_gradient = (probs * (d_probs - delta[..., None]) * scale).astype(jnp.bfloat16)
        dq_b = jnp.einsum(
            "gij,jd->igd", scores_gradient, key_block_tile, preferred_element_type=jnp.float32
        ).astype(jnp.bfloat16)
        key_terms.append(
            jnp.einsum(
                "gij,igd->jd", scores_gradient, query_block_tile, preferred_element_type=jnp.float32
            )
        )
        value_terms.append(
            jnp.einsum(
                "gij,igd->jd", probability_block, delta_block, preferred_element_type=jnp.float32
            )
        )
        out_parts.append(out_b.reshape(row_count, heads_per_group * HEAD_WIDTH))
        dq_parts.append(dq_b.reshape(row_count, heads_per_group * HEAD_WIDTH))
    return (
        jnp.concatenate(out_parts, axis=1),
        jnp.concatenate(dq_parts, axis=1),
        jnp.concatenate(key_terms, axis=1),
        jnp.concatenate(value_terms, axis=1),
    )


def cut_windows(whole, seg_rows):
    segments = whole.reshape(-1, seg_rows, whole.shape[-1])
    return jnp.concatenate([segments[:-2], segments[1:-1], segments[2:]], axis=1)


def fold_tiles(windows, seg_rows):
    count = windows.shape[0]
    columns = windows.shape[-1]
    tiles = windows.reshape(count, 3, seg_rows, columns)
    total = jnp.zeros((count + 2, seg_rows, columns), jnp.float32)
    for tile in range(3):
        total = total + jnp.pad(tiles[:, tile], ((tile, 2 - tile), (0, 0), (0, 0)))
    return total.reshape((count + 2) * seg_rows, columns)


def on_device(
    query_matrix, key_matrix, value_matrix, output_gradient, document_length_list, slab_plan
):
    rows_dev = query_matrix.shape[0]
    ctx_size = lax.axis_size("ctx")
    slab_rows = rows_dev // ctx_size
    group_len = rows_dev * ctx_size
    margin = 2 * rows_dev
    group_idx = lax.axis_index("dp")
    place = lax.axis_index("ctx")
    offset = group_idx * group_len
    plan_grid = slab_plan[0]
    owners = jnp.arange(ctx_size, dtype=jnp.int32)
    slab_ids = jnp.arange(slab_rows, dtype=jnp.int32)
    window_ids = jnp.arange(3 * rows_dev, dtype=jnp.int32)
    group_k_pos = offset + owners[:, None] * rows_dev - margin + window_ids[None, :]
    my_slabs = plan_grid[place]
    send_q = jnp.take(query_matrix.reshape(ctx_size, slab_rows, -1), my_slabs, axis=0)
    send_d = jnp.take(output_gradient.reshape(ctx_size, slab_rows, -1), my_slabs, axis=0)
    got_q, got_d = (
        lax.all_to_all(send_q, "ctx", split_axis=0, concat_axis=0, tiled=True),
        lax.all_to_all(send_d, "ctx", split_axis=0, concat_axis=0, tiled=True),
    )
    q_pos = (
        offset
        + owners[:, None] * rows_dev
        + plan_grid[:, place][:, None] * slab_rows
        + slab_ids[None, :]
    )
    whole_k, whole_v = (
        lax.all_gather(key_matrix, "ctx", axis=0, tiled=True),
        lax.all_gather(value_matrix, "ctx", axis=0, tiled=True),
    )
    prior_k, prior_v = shifted((whole_k[-margin:], whole_v[-margin:]), "dp", 1)
    win_k = cut_windows(jnp.concatenate([prior_k, whole_k], axis=0), rows_dev)
    win_v = cut_windows(jnp.concatenate([prior_v, whole_v], axis=0), rows_dev)
    single_span = partial(
        attend_over_span, document_length_list=document_length_list, key_value_count=KEY_VALUE_HEADS
    )
    out_b, dq_b, dk_b, dv_b = jax.vmap(single_span)(got_q, got_d, q_pos, win_k, win_v, group_k_pos)
    attended = out_b.reshape(rows_dev, -1)
    query_grads = dq_b.reshape(rows_dev, -1)
    dk_all = fold_tiles(dk_b, rows_dev)
    dv_all = fold_tiles(dv_b, rows_dev)
    back_k, back_v = shifted((dk_all[:margin], dv_all[:margin]), "dp", -1)
    own_k = dk_all[margin:].at[-margin:].add(back_k)
    own_v = dv_all[margin:].at[-margin:].add(back_v)
    summed_k, summed_v = (
        lax.psum_scatter(own_k, "ctx", scatter_dimension=0, tiled=True),
        lax.psum_scatter(own_v, "ctx", scatter_dimension=0, tiled=True),
    )
    return (attended, query_grads, summed_k.astype(jnp.bfloat16), summed_v.astype(jnp.bfloat16))


def solution(mesh):
    placed = (
        P(("dp", "ctx"), None),
        P(("dp", "ctx"), None),
        P(("dp", "ctx"), None),
        P(("dp", "ctx"), None),
        P(),
        P("dp", None, None),
    )
    return jax.shard_map(
        on_device,
        mesh=mesh,
        in_specs=placed,
        out_specs=(
            P(("dp", "ctx"), None),
            P(("dp", "ctx"), None),
            P(("dp", "ctx"), None),
            P(("dp", "ctx"), None),
        ),
        check_vma=False,
    )
```

profile of v0, /device:TPU:7, one launch (start us, length us, event | category | flops | bytes accessed | tf_op | source)
XLA Modules:
  0.0 370.2 jit_solution(15736168992870357533)
XLA Ops:
  7.2 0.7 all-gather.3.cloned.1.call-update
  8.0 0.7 all-gather.5.cloned.1.call-update
  8.7 0.7 compare_and_fusion.1
  10.7 1.6 broadcast_select_fusion
  12.2 7.9 %all-to-all-start = ((bf16[16,8,4096]{2,1,0:T(8,128)(2,1)}), bf16[16,8,4096]{2,1,0:T(8,128)(2,1)S(1)}, u32[]{:S(2)}, u32[]{:S(2)}) async-start(bf16[16,8,4096]{2,1,0:T(8,128)(2,1)} %get-tuple-element.58), calls=%async_computation | async-start | bytes 2097152 | tf_op jit(solution)/shard_map/all_to_all | solution.py:125
  20.7 16.3 %all-to-all-done = bf16[16,8,4096]{2,1,0:T(8,128)(2,1)S(1)} async-done(((bf16[16,8,4096]{2,1,0:T(8,128)(2,1)}), bf16[16,8,4096]{2,1,0:T(8,128)(2,1)S(1)}, u32[]{:S(2)}, u32[]{:S(2)}) %all-to-all-start) | async-done | bytes 1048608 | tf_op jit(solution)/shard_map/all_to_all | solution.py:125
  37.1 4.1 %all-to-all-start.1 = ((bf16[16,8,4096]{2,1,0:T(8,128)(2,1)}), bf16[16,8,4096]{2,1,0:T(8,128)(2,1)S(1)}, u32[]{:S(2)}, u32[]{:S(2)}) async-start(bf16[16,8,4096]{2,1,0:T(8,128)(2,1)} %get-tuple-element.57), calls=%async_computation.1 | async-start | bytes 2097152 | tf_op jit(solution)/shard_map/all_to_all | solution.py:126
  41.9 24.9 %all-gather.3.cloned.1.call-done = bf16[2048,512]{1,0:T(8,128)(2,1)} async-done(((bf16[128,512]{1,0:T(8,128)(2,1)}), bf16[2048,512]{1,0:T(8,128)(2,1)}) %all-gather.3.cloned.1.call-update) | async-done | bytes 2097168 | tf_op jit(solution)/shard_map/all_gather | solution.py:136
  66.9 1.7 slice.218
  68.5 1.3 collective-permute-start
  69.8 0.9 slice_bitcast_fusion.45
  70.7 1.0 slice_bitcast_fusion.41
  71.7 41.7 %all-gather.5.cloned.1.call-done = bf16[2048,512]{1,0:T(8,128)(2,1)} async-done(((bf16[128,512]{1,0:T(8,128)(2,1)}), bf16[2048,512]{1,0:T(8,128)(2,1)}) %all-gather.5.cloned.1.call-update) | async-done | bytes 2097168 | tf_op jit(solution)/shard_map/all_gather | solution.py:135
  113.5 1.0 slice.222
  114.4 1.3 collective-permute-start.1
  115.8 1.0 constant_dynamic-update-slice_fusion.1
  117.3 1.8 collective-permute-done.1
  119.7 4.8 %pad_maximum_fusion.3 = bf16[16,384,512]{2,1,0:T(8,128)(2,1)S(1)} fusion(bf16[16,128,512]{2,1,0:T(8,128)(2,1)S(1)} %bitcast.282, bf16[16,128,512]{2,1,0:T(8,128)(2,1)S(1)} %bitcast.286, bf16[16,128,512]{2,1,0:T(8,128)(2,1)S(1)} %bitcast.285), kind=kLoop, calls=%fused_computation.5 | loop fusion | flops 18874368 | bytes 12582912 | tf_op jit(solution)/shard_map/concatenate | solution.py:92
  124.5 0.9 fusion.57
  126.4 0.7 copy-done.11
  127.1 0.9 fusion.58
  129.2 4.9 %pad_maximum_fusion.2 = bf16[16,384,512]{2,1,0:T(8,128)(2,1)S(1)} fusion(bf16[16,128,512]{2,1,0:T(8,128)(2,1)S(1)} %bitcast.281, bf16[16,128,512]{2,1,0:T(8,128)(2,1)S(1)} %bitcast.284, bf16[16,128,512]{2,1,0:T(8,128)(2,1)S(1)} %bitcast.283), kind=kLoop, calls=%fused_computation.4 | loop fusion | flops 18874368 | bytes 12582912 | tf_op jit(solution)/shard_map/concatenate | solution.py:92
  135.5 0.9 fusion.59
  138.9 0.9 fusion.60
  140.9 0.6 copy-done.45
  141.9 2.0 multiply_reduce_fusion.3
  143.9 0.9 copy.109
  144.8 1.6 copy.118
  146.3 1.6 copy.115
  147.9 1.5 copy.112
  149.4 2.9 fusion.11
  152.4 1.9 convolution_bitcast_fusion.7
  154.4 0.8 fusion.2
  156.2 0.8 copy-done.14
  157.0 0.8 fusion.5
  158.0 0.6 convolution_bitcast_fusion.5
  159.2 0.8 fusion.8
  160.1 0.9 copy-done.41
  161.6 5.2 %pad_maximum_fusion = f32[16,384,512]{1,2,0:T(8,128)} fusion(f32[16,384,128]{1,2,0:T(8,128)S(1)} %convolution_bitcast_fusion.4, f32[16,384,128]{1,2,0:T(8,128)S(1)} %convolution_bitcast_fusion.5, f32[16,384,128]{1,2,0:T(8,128)S(1)} %convolution_bitcast_fusion.6, f32[16,384,128]{1,2,0:T(8,128)S(1)} %convolution_bitcast_fusion.7), kind=kLoop, calls=%fused_computation.2 | loop fusion | flops 9437184 | bytes 25165824 | tf_op jit(solution)/shard_map/vmap()/concatenate | solution.py:85
  166.7 12.7 %copy.120 = f32[16,384,512]{2,1,0:T(8,128)} copy(f32[16,384,512]{1,2,0:T(8,128)} %pad_maximum_fusion) | data formatting | bytes 25165824 | tf_op jit(solution)/shard_map/vmap()/concatenate | solution.py:85
  179.4 10.1 %slice_bitcast_fusion.5 = (f32[16,128,512]{2,1,0:T(8,128)S(1)}, f32[16,128,512]{2,1,0:T(8,128)}, f32[16,128,512]{2,1,0:T(8,128)}) fusion(f32[16,3,128,512]{3,2,1,0:T(8,128)} %bitcast.279), kind=kLoop, calls=%fused_computation.13 | loop fusion | bytes 25165824 | tf_op jit(solution)/shard_map/squeeze | solution.py:101
  189.5 1.5 pad_add_fusion.5
  190.9 7.0 %collective-permute-start.2 = (f32[256,512]{1,0:T(8,128)S(1)}, f32[256,512]{1,0:T(8,128)S(1)}, u32[]{:S(2)}, u32[]{:S(2)}) collective-permute-start(f32[256,512]{1,0:T(8,128)S(1)} %bitcast.290), channel_id=1, source_target_pairs={{16,0},{32,16},{48,32},{64,48},{80,64},{96,80},{112,96},{17,1},{33... | collective-permute-start | bytes 1572872 | tf_op jit(solution)/shard_map/ppermute | solution.py:16
  197.9 1.8 pad_add_fusion.1
  199.8 2.4 slice.243
  202.2 0.9 constant_dynamic-update-slice_fusion.5
  207.3 5.2 %pad_maximum_fusion.1 = f32[16,384,512]{1,2,0:T(8,128)} fusion(f32[16,384,128]{1,2,0:T(8,128)S(1)} %convolution_bitcast_fusion, f32[16,384,128]{1,2,0:T(8,128)S(1)} %convolution_bitcast_fusion.1, f32[16,384,128]{1,2,0:T(8,128)S(1)} %convolution_bitcast_fusion.2, f32[16,384,128]{1,2,0:T(8,128)S(1)} %convolution_bitcast_fusion.3), kind=kLoop, calls=%fused_computation.3 | loop fusion | flops 9437184 | bytes 25165824 | tf_op jit(solution)/shard_map/vmap()/concatenate | solution.py:86
  212.4 12.7 %copy.127 = f32[16,384,512]{2,1,0:T(8,128)} copy(f32[16,384,512]{1,2,0:T(8,128)} %pad_maximum_fusion.1) | data formatting | bytes 25165824 | tf_op jit(solution)/shard_map/vmap()/concatenate | solution.py:86
  225.1 10.5 %slice_bitcast_fusion.2 = (f32[16,128,512]{2,1,0:T(8,128)S(1)}, f32[16,128,512]{2,1,0:T(8,128)}, f32[16,128,512]{2,1,0:T(8,128)}) fusion(f32[16,3,128,512]{3,2,1,0:T(8,128)} %bitcast.280), kind=kLoop, calls=%fused_computation.10 | loop fusion | bytes 25165824 | tf_op jit(solution)/shard_map/squeeze | solution.py:101
  235.6 1.5 pad_add_fusion.3
  237.1 4.7 %collective-permute-start.3 = (f32[256,512]{1,0:T(8,128)S(1)}, f32[256,512]{1,0:T(8,128)S(1)}, u32[]{:S(2)}, u32[]{:S(2)}) collective-permute-start(f32[256,512]{1,0:T(8,128)S(1)} %bitcast.291), channel_id=1, source_target_pairs={{16,0},{32,16},{48,32},{64,48},{80,64},{96,80},{112,96},{17,1},{33... | collective-permute-start | bytes 1572872 | tf_op jit(solution)/shard_map/ppermute | solution.py:16
  241.9 1.8 pad_add_fusion
  243.7 2.4 slice.247
  246.1 0.9 constant_dynamic-update-slice_fusion.4
  247.0 1.1 copy-done.42
  248.2 2.0 fusion.17
  250.2 1.9 fusion.18
  252.6 0.7 copy-done.36
  253.7 1.0 pad_maximum_fusion.5
  255.3 1.0 pad_maximum_fusion.4
  256.3 25.2 %reduce-scatter.3.cloned.1.call-done = f32[128,512]{1,0:T(8,128)} async-done(((f32[2048,512]{1,0:T(8,128)}), f32[128,512]{1,0:T(8,128)}) %reduce-scatter.3.cloned.1.call-update) | async-done | bytes 262160 | tf_op jit(solution)/shard_map/reduce_scatter | solution.py:153
  281.6 1.6 convert_element_type.143
  283.2 78.9 %reduce-scatter.5.cloned.1.call-done = f32[128,512]{1,0:T(8,128)} async-done(((f32[2048,512]{1,0:T(8,128)}), f32[128,512]{1,0:T(8,128)}) %reduce-scatter.5.cloned.1.call-update) | async-done | bytes 262160 | tf_op jit(solution)/shard_map/reduce_scatter | solution.py:154
  362.1 1.6 convert_element_type.144
  (169 shorter events, 18.8 us)
Async XLA Ops:
  7.2 2.2 copy-start
  7.2 2.8 copy-start.22
  7.2 59.7 %all-gather.3.cloned.1.call-start = ((), (), s32[]{:S(2)}) async-start(), calls=%async_computation.4 | async-start | bytes 2228224 | tf_op jit(solution)/shard_map/all_gather | solution.py:136
  7.9 105.6 %all-gather.5.cloned.1.call-start = ((), (), s32[]{:S(2)}) async-start(), calls=%async_computation.5 | async-start | bytes 2228224 | tf_op jit(solution)/shard_map/all_gather | solution.py:135
  12.2 7.9 %copy-start.59 = (s32[96]{0:T(128)S(1)}, s32[96]{0:T(128)}, u32[]{:S(2)}) copy-start(s32[96]{0:T(128)} %param.16) | copy-start | bytes 1156
  12.2 8.3 %copy-start.58 = (s32[1,16,16]{2,1,0:T(8,128)S(1)}, s32[1,16,16]{2,1,0:T(8,128)}, u32[]{:S(2)}) copy-start(s32[1,16,16]{2,1,0:T(8,128)} %param.17) | copy-start | bytes 3076
  12.2 24.8 %all-to-all-start = ((bf16[16,8,4096]{2,1,0:T(8,128)(2,1)}), bf16[16,8,4096]{2,1,0:T(8,128)(2,1)S(1)}, u32[]{:S(2)}, u32[]{:S(2)}) async-start(bf16[16,8,4096]{2,1,0:T(8,128)(2,1)} %get-tuple-element.58), calls=%async_computation | async-start | bytes 2097152 | tf_op jit(solution)/shard_map/all_to_all | solution.py:125
  37.1 33.7 %all-to-all-start.1 = ((bf16[16,8,4096]{2,1,0:T(8,128)(2,1)}), bf16[16,8,4096]{2,1,0:T(8,128)(2,1)S(1)}, u32[]{:S(2)}, u32[]{:S(2)}) async-start(bf16[16,8,4096]{2,1,0:T(8,128)(2,1)} %get-tuple-element.57), calls=%async_computation.1 | async-start | bytes 2097152 | tf_op jit(solution)/shard_map/all_to_all | solution.py:126
  41.2 240.4 %reduce-scatter.3.cloned.1.call-start = ((), (), s32[]{:S(2)}) async-start(), calls=%async_computation.6 | async-start | bytes 4456448 | tf_op jit(solution)/shard_map/reduce_scatter | solution.py:153
  41.9 85.2 %copy-start.56 = (pred[16,8,384]{2,1,0:T(8,128)(4,1)}, pred[16,8,384]{2,1,0:T(8,128)(4,1)S(1)}, u32[]{:S(2)}) copy-start(pred[16,8,384]{2,1,0:T(8,128)(4,1)S(1)} %compare_and_fusion) | copy-start | bytes 147460
  68.5 47.2 %collective-permute-start = (bf16[256,512]{1,0:T(8,128)(2,1)}, bf16[256,512]{1,0:T(8,128)(2,1)}, u32[]{:S(2)}, u32[]{:S(2)}) collective-permute-start(bf16[256,512]{1,0:T(8,128)(2,1)} %slice.218), channel_id=1, source_target_pairs={{0,16},{16,32},{32,48},{48,64},{64,80},{80,96},{96,112},{1,17},{17... | collective-permute-start | bytes 786440 | tf_op jit(solution)/shard_map/ppermute | solution.py:16
  70.7 64.3 %copy-start.28 = (bf16[16,8,8,128]{3,1,2,0:T(8,128)(2,1)}, bf16[16,8,8,128]{3,1,2,0:T(8,128)(2,1)S(1)}, u32[]{:S(2)}) copy-start(bf16[16,8,8,128]{3,1,2,0:T(8,128)(2,1)S(1)} %get-tuple-element.56) | copy-start | bytes 786436
  70.7 46.0 %copy-start.6 = (bf16[2048,512]{1,0:T(8,128)(2,1)S(1)}, bf16[2048,512]{1,0:T(8,128)(2,1)}, u32[]{:S(2)}) copy-start(bf16[2048,512]{1,0:T(8,128)(2,1)} %all-gather.3.cloned.1.call-done) | copy-start | bytes 6291460
  114.4 4.7 %collective-permute-start.1 = (bf16[256,512]{1,0:T(8,128)(2,1)S(1)}, bf16[256,512]{1,0:T(8,128)(2,1)S(1)}, u32[]{:S(2)}, u32[]{:S(2)}) collective-permute-start(bf16[256,512]{1,0:T(8,128)(2,1)S(1)} %slice.222), channel_id=1, source_target_pairs={{0,16},{16,32},{32,48},{48,64},{64,80},{80,96},{96,112},{1,17},{17... | collective-permute-start | bytes 786440 | tf_op jit(solution)/shard_map/ppermute | solution.py:16
  116.9 2.2 copy-start.7
  119.6 4.8 %copy-start.32 = (bf16[16,8,8,128]{3,1,2,0:T(8,128)(2,1)S(1)}, bf16[16,8,8,128]{3,1,2,0:T(8,128)(2,1)}, u32[]{:S(2)}) copy-start(bf16[16,8,8,128]{3,1,2,0:T(8,128)(2,1)} %get-tuple-element.54) | copy-start | bytes 786436
  124.5 13.9 %copy-start.8 = (bf16[16,384,512]{2,1,0:T(8,128)(2,1)}, bf16[16,384,512]{2,1,0:T(8,128)(2,1)S(1)}, u32[]{:S(2)}) copy-start(bf16[16,384,512]{2,1,0:T(8,128)(2,1)S(1)} %pad_maximum_fusion.3) | copy-start | bytes 18874372
  125.4 1.7 copy-start.11
  125.4 1.7 copy-start.30
  127.1 7.1 %copy-start.16 = (bf16[16,8,8,384]{3,1,2,0:T(8,128)(2,1)}, bf16[16,8,8,384]{3,1,2,0:T(8,128)(2,1)S(1)}, u32[]{:S(2)}) copy-start(bf16[16,8,8,384]{3,1,2,0:T(8,128)(2,1)S(1)} %fusion.15) | copy-start | bytes 2359300
  128.0 1.2 copy-start.13
  129.2 5.4 %copy-start.18 = (bf16[16,8,8,384]{3,1,2,0:T(8,128)(2,1)}, bf16[16,8,8,384]{3,1,2,0:T(8,128)(2,1)S(1)}, u32[]{:S(2)}) copy-start(bf16[16,8,8,384]{3,1,2,0:T(8,128)(2,1)S(1)} %fusion.14) | copy-start | bytes 2359300
  134.2 7.6 %copy-start.9 = (bf16[16,384,512]{2,1,0:T(8,128)(2,1)}, bf16[16,384,512]{2,1,0:T(8,128)(2,1)S(1)}, u32[]{:S(2)}) copy-start(bf16[16,384,512]{2,1,0:T(8,128)(2,1)S(1)} %pad_maximum_fusion.2) | copy-start | bytes 18874372
  134.6 7.2 %copy-start.46 = (bf16[16,128,8,8]{1,3,2,0:T(8,128)(2,1)}, bf16[16,128,8,8]{1,3,2,0:T(8,128)(2,1)S(1)}, u32[]{:S(2)}) copy-start(bf16[16,128,8,8]{1,3,2,0:T(8,128)(2,1)S(1)} %convolution_convert_fusion.4) | copy-start | bytes 786436
  135.1 6.8 %copy-start.48 = (bf16[16,128,8,8]{1,3,2,0:T(8,128)(2,1)}, bf16[16,128,8,8]{1,3,2,0:T(8,128)(2,1)S(1)}, u32[]{:S(2)}) copy-start(bf16[16,128,8,8]{1,3,2,0:T(8,128)(2,1)S(1)} %convolution_convert_fusion.5) | copy-start | bytes 786436
  137.9 1.0 copy-start.34
  138.3 3.5 copy-start.50
  139.7 1.1 copy-start.15
  141.9 2.0 copy-start.20
  149.4 4.9 %copy-start.10 = (bf16[16,384,512]{2,1,0:T(8,128)(2,1)S(1)}, bf16[16,384,512]{2,1,0:T(8,128)(2,1)}, u32[]{:S(2)}) copy-start(bf16[16,384,512]{2,1,0:T(8,128)(2,1)} %copy-done.9) | copy-start | bytes 18874372
  152.4 1.9 copy-start.35
  152.4 2.0 copy-start.12
  152.4 2.0 copy-start.24
  152.4 2.0 copy-start.55
  155.3 1.7 copy-start.14
  155.3 1.7 copy-start.26
  155.3 1.7 copy-start.54
  158.0 1.1 copy-start.27
  158.0 1.2 copy-start.44
  158.0 1.2 copy-start.53
  159.2 1.7 copy-start.29
  189.5 8.4 %copy-start.2 = (f32[16,128,512]{2,1,0:T(8,128)S(1)}, f32[16,128,512]{2,1,0:T(8,128)}, u32[]{:S(2)}) copy-start(f32[16,128,512]{2,1,0:T(8,128)} %get-tuple-element.43) | copy-start | bytes 12582916
  189.5 8.5 %copy-start.3 = (f32[16,128,512]{2,1,0:T(8,128)S(1)}, f32[16,128,512]{2,1,0:T(8,128)}, u32[]{:S(2)}) copy-start(f32[16,128,512]{2,1,0:T(8,128)} %get-tuple-element.44) | copy-start | bytes 12582916
  190.9 11.2 %collective-permute-start.2 = (f32[256,512]{1,0:T(8,128)S(1)}, f32[256,512]{1,0:T(8,128)S(1)}, u32[]{:S(2)}, u32[]{:S(2)}) collective-permute-start(f32[256,512]{1,0:T(8,128)S(1)} %bitcast.290), channel_id=1, source_target_pairs={{16,0},{32,16},{48,32},{64,48},{80,64},{96,80},{112,96},{17,1},{33... | collective-permute-start | bytes 1572872 | tf_op jit(solution)/shard_map/ppermute | solution.py:16
  203.1 1.1 copy-start.19
  203.1 158.9 %reduce-scatter.5.cloned.1.call-start = ((), (), s32[]{:S(2)}) async-start(), calls=%async_computation.7 | async-start | bytes 4456448 | tf_op jit(solution)/shard_map/reduce_scatter | solution.py:154
  204.3 1.1 copy-start.17
  204.3 1.2 copy-start.25
  205.5 1.1 copy-start.21
  205.5 1.2 copy-start.23
  235.6 6.3 %copy-start.4 = (f32[16,128,512]{2,1,0:T(8,128)S(1)}, f32[16,128,512]{2,1,0:T(8,128)}, u32[]{:S(2)}) copy-start(f32[16,128,512]{2,1,0:T(8,128)} %get-tuple-element.38) | copy-start | bytes 12582916
  235.6 6.3 %copy-start.5 = (f32[16,128,512]{2,1,0:T(8,128)S(1)}, f32[16,128,512]{2,1,0:T(8,128)}, u32[]{:S(2)}) copy-start(f32[16,128,512]{2,1,0:T(8,128)} %get-tuple-element.39) | copy-start | bytes 12582916
  237.1 9.0 %collective-permute-start.3 = (f32[256,512]{1,0:T(8,128)S(1)}, f32[256,512]{1,0:T(8,128)S(1)}, u32[]{:S(2)}, u32[]{:S(2)}) collective-permute-start(f32[256,512]{1,0:T(8,128)S(1)} %bitcast.291), channel_id=1, source_target_pairs={{16,0},{32,16},{48,32},{64,48},{80,64},{96,80},{112,96},{17,1},{33... | collective-permute-start | bytes 1572872 | tf_op jit(solution)/shard_map/ppermute | solution.py:16
  247.0 1.1 copy-start.42
  247.0 5.1 %slice-start = ((s8[6291456]{0:T(1024)(128)(4,1)}), s8[2097152]{0:T(1024)(128)(4,1)S(1)}, s32[]{:S(2)}) async-start(s8[6291456]{0:T(1024)(128)(4,1)} %bitcast.287), calls=%async_computation.8 | async-start | bytes 4194304
  248.1 2.0 copy-start.40
  248.1 4.0 %slice-start.1 = ((s8[6291456]{0:T(1024)(128)(4,1)}), s8[4194304]{0:T(1024)(128)(4,1)S(1)}, s32[]{:S(2)}) async-start(s8[6291456]{0:T(1024)(128)(4,1)} %bitcast.287), calls=%async_computation.9 | async-start | bytes 8388608
  250.2 2.0 copy-start.38
  252.1 1.1 copy-start.36
  253.3 110.4 %copy-start.1 = (bf16[128,4096]{1,0:T(8,128)(2,1)S(1)}, bf16[128,4096]{1,0:T(8,128)(2,1)}, u32[]{:S(2)}) copy-start(bf16[128,4096]{1,0:T(8,128)(2,1)} %param.15) | copy-start | bytes 3145732
  253.7 1.1 copy-start.47
  253.7 1.1 copy-start.49
  253.7 1.4 copy-start.51
  253.7 1.6 copy-start.52
  (8 other events, 6.7 us)
Sparse Core Ops, SparseCore 0:
  10.2 56.6 all-gather.2
  69.0 44.4 all-gather.4
  203.3 78.2 reduce-scatter.2
  285.1 76.9 reduce-scatter.4
where the time goes:
time: 374 us; the launch traced here: 370 us
  waiting for transfers between devices  190 us (51%)
  local copies, waits for them, and re-layouts  74.8 us (20%)
  other arithmetic  40.9 us (11%)
  starting transfers between devices  26.4 us (7%)
  matrix products  23.1 us (6%)
  between operations  14.6 us (4%)
    reduce_scatter x1, waiting for transfers between devices, on_device(): lax.psum_scatter(own_v, 'ctx', scatter_dimension=0, tiled=True)  78.9 us
    all_gather x1, waiting for transfers between devices, on_device(): lax.all_gather(key_matrix, 'ctx', axis=0, tiled=True)  41.7 us
    reduce_scatter x1, waiting for transfers between devices, on_device(): lax.psum_scatter(own_k, 'ctx', scatter_dimension=0, tiled=True)  25.2 us
    all_gather x1, waiting for transfers between devices, on_device(): lax.all_gather(value_matrix, 'ctx', axis=0, tiled=True)  24.9 us
    squeeze x2, local copies, waits for them, and re-layouts, fold_tiles(): total = total + jnp.pad(tiles[:, tile], ((tile, 2 - tile), (0, 0), (0, 0)))  20.5 us
    all_to_all x1, waiting for transfers between devices, on_device(): lax.all_to_all(send_q, 'ctx', split_axis=0, concat_axis=0, tiled=True)  16.3 us
    ppermute x4, starting transfers between devices, shifted(): return lax.ppermute(x, axis, pairs)  14.3 us
    concatenate x1, local copies, waits for them, and re-layouts, attend_over_span(): jnp.concatenate(value_terms, axis=1)  12.7 us
  transfers between devices with their start and end apart: 10, of which 6 were waited for; matrix products, arithmetic and copies ran while one was open for 16% of the time, Pallas kernels for 0%

commit v1 on v0

v1 whole, which is shorter than its diff:
```python
import functools
import math

import jax
import jax.numpy as jnp
from jax import lax
from jax.experimental import pallas as pl
from jax.experimental.pallas import tpu as pltpu
from jax.sharding import PartitionSpec as P

KV = 4
W = 128
PER = 8
ROWS = 128
SPLIT = 16
SLAB = ROWS // SPLIT
GROUPS = 8
DOCS = 96
PAIR = 2
MESH = pl.DeviceIdType.MESH
NT = (((1,), (1,)), ((), ()))
SCALE = 1.0 / math.sqrt(W)
LOG2E = math.log2(math.e)


def dot(a, b):
    return jnp.dot(a, b, preferred_element_type=jnp.float32)


def dot_nt(a, b):
    return lax.dot_general(a, b, NT, preferred_element_type=jnp.float32)


def kernel(
    q_hbm, do_hbm, k_hbm, v_hbm, doc_hbm, plan_hbm,
    att_ref, dq_ref, dk_ref, dv_ref,
    q_v, do_v, k_v, v_v, doc_s, plan_s, halo, sendb, recvb, gsend, grecv, own, bias, perm,
    load_sem, small_sem, hsend, hrecv, asend, arecv, aself, gs_sem, gr_sem,
):
    g, c = lax.axis_index("dp"), lax.axis_index("ctx")
    line = g * SPLIT + c
    total = GROUPS * SPLIT

    def along(by):
        other = (line + by + total) % total
        return (other // SPLIT, other % SPLIT)

    barrier = pltpu.get_barrier_semaphore()
    for by in (1, 2, -1, -2):
        pl.semaphore_signal(barrier, inc=1, device_id=along(by), device_id_type=MESH)

    def greet(k, _):
        pl.semaphore_signal(barrier, inc=1, device_id=(g, (c + k) % SPLIT), device_id_type=MESH)
        return 0

    lax.fori_loop(1, SPLIT, greet, 0)

    loads = [
        pltpu.make_async_copy(src, dst, load_sem.at[i])
        for i, (src, dst) in enumerate(((q_hbm, q_v), (do_hbm, do_v), (k_hbm, k_v), (v_hbm, v_v)))
    ]
    smalls = [
        pltpu.make_async_copy(doc_hbm, doc_s, small_sem.at[0]),
        pltpu.make_async_copy(plan_hbm.at[0], plan_s, small_sem.at[1]),
    ]
    for copy in smalls + loads:
        copy.start()

    for copy in smalls:
        copy.wait()
    pos = line * ROWS + lax.broadcasted_iota(jnp.int32, (1, ROWS), 1)

    def add_doc(i, carry):
        end, first = carry
        length = doc_s[i]
        end = end + length
        return end, first + jnp.where(end <= pos, length, 0)

    _, first = lax.fori_loop(0, DOCS, add_doc, (jnp.int32(0), jnp.zeros((1, ROWS), jnp.int32)))
    k_pos = line * ROWS - 2 * ROWS + lax.broadcasted_iota(jnp.int32, (3 * ROWS, ROWS), 0)
    bias[...] = jnp.where((k_pos >= first) & (k_pos <= pos), 0.0, -1e30).astype(jnp.float32)

    r_id = lax.broadcasted_iota(jnp.int32, (2 * SLAB, 2 * ROWS), 0)
    r_id = jnp.where(r_id >= SLAB, r_id - SLAB + ROWS, r_id)
    column = lax.broadcasted_iota(jnp.int32, (2 * SLAB, 2 * ROWS), 1)
    for d in range(SPLIT):
        hit = column == r_id + plan_s[c, d] * SLAB
        perm[d * 2 * SLAB : (d + 1) * 2 * SLAB, :] = jnp.where(hit, 1.0, 0.0).astype(jnp.bfloat16)
    eye = jnp.where(
        lax.broadcasted_iota(jnp.int32, (W, W), 0) == lax.broadcasted_iota(jnp.int32, (W, W), 1),
        1.0,
        0.0,
    ).astype(jnp.bfloat16)

    pl.semaphore_wait(barrier, SPLIT - 1 + 4)

    for h in range(KV):
        for i, src in enumerate((k_hbm, v_hbm)):
            for by in (1, 2):
                pltpu.make_async_remote_copy(
                    src_ref=src.at[:, pl.ds(h * W, W)],
                    dst_ref=halo.at[h, i, pl.ds((2 - by) * ROWS, ROWS)],
                    send_sem=hsend,
                    recv_sem=hrecv.at[h],
                    device_id=along(by),
                    device_id_type=MESH,
                ).start()
    for copy in loads:
        copy.wait()

    def one_head(h, _):
        pltpu.make_async_copy(halo.at[h], halo.at[h], hrecv.at[h]).wait()
        kcol = pl.ds(pl.multiple_of(h * W, W), W)
        kw = jnp.concatenate([halo[h, 0], k_v[:, kcol]], axis=0)
        vw = jnp.concatenate([halo[h, 1], v_v[:, kcol]], axis=0)
        kt = dot_nt(eye, kw).astype(jnp.bfloat16)
        vt = dot_nt(eye, vw).astype(jnp.bfloat16)
        mask = jnp.concatenate([bias[...]] * PAIR, axis=1)
        dk = jnp.zeros((3 * ROWS, W), jnp.float32)
        dv = jnp.zeros((3 * ROWS, W), jnp.float32)
        for p in range(PER // PAIR):
            base = h * (PER * W) + p * PAIR * W
            cols = [pl.ds(pl.multiple_of(base + s * W, W), W) for s in range(PAIR)]
            qs = jnp.concatenate([q_v[:, s] for s in cols], axis=0)
            dos = jnp.concatenate([do_v[:, s] for s in cols], axis=0)
            scores = dot_nt(kw, qs) + mask
            top = jnp.max(scores, axis=0, keepdims=True)
            e = jnp.exp2((scores - top) * (SCALE * LOG2E))
            inv = 1.0 / jnp.sum(e, axis=0, keepdims=True)
            d_probs = dot_nt(vw, dos)
            probs = e * inv
            delta = jnp.sum(probs * d_probs, axis=0, keepdims=True)
            pb = probs.astype(jnp.bfloat16)
            ds = (probs * (d_probs - delta)).astype(jnp.bfloat16)
            dv = dv + dot(pb, dos)
            dk = dk + dot(ds, qs)
            out_t = dot(vt, pb).astype(jnp.bfloat16)
            dq_t = (dot(kt, ds) * SCALE).astype(jnp.bfloat16)
            for s in range(PAIR):
                both = jnp.concatenate(
                    [out_t[:, s * ROWS : (s + 1) * ROWS], dq_t[:, s * ROWS : (s + 1) * ROWS]], axis=1
                )
                message = dot_nt(perm[...], both).astype(jnp.bfloat16)
                sendb[:, :, cols[s]] = message.reshape(SPLIT, 2 * SLAB, W)
            span = pl.ds(pl.multiple_of(base, W), PAIR * W)

            def send(k, _, span=span):
                d = (c + k) % SPLIT
                pltpu.make_async_remote_copy(
                    src_ref=sendb.at[d, :, span],
                    dst_ref=recvb.at[c, :, span],
                    send_sem=asend,
                    recv_sem=arecv.at[h],
                    device_id=(g, d),
                    device_id_type=MESH,
                ).start()
                return 0

            lax.fori_loop(1, SPLIT, send, 0)
        dk = dk * SCALE
        own[h, 0] = dk[2 * ROWS :]
        own[h, 1] = dv[2 * ROWS :]
        gsend[h, 0, 0] = dk[ROWS : 2 * ROWS].astype(jnp.bfloat16)
        gsend[h, 0, 1] = dv[ROWS : 2 * ROWS].astype(jnp.bfloat16)
        gsend[h, 1, 0] = dk[:ROWS].astype(jnp.bfloat16)
        gsend[h, 1, 1] = dv[:ROWS].astype(jnp.bfloat16)
        for by in (1, 2):
            pltpu.make_async_remote_copy(
                src_ref=gsend.at[h, by - 1],
                dst_ref=grecv.at[h, by - 1],
                send_sem=gs_sem,
                recv_sem=gr_sem.at[h],
                device_id=along(-by),
                device_id_type=MESH,
            ).start()
        wide = pl.ds(pl.multiple_of(h * PER * W, W), PER * W)
        pltpu.make_async_copy(sendb.at[c, :, wide], recvb.at[c, :, wide], aself.at[h]).start()
        return 0

    lax.fori_loop(0, KV, one_head, 0)

    def finish(h, _):
        kcol = pl.ds(pl.multiple_of(h * W, W), W)
        wide = pl.ds(pl.multiple_of(h * PER * W, W), PER * W)
        pltpu.make_async_copy(grecv.at[h], grecv.at[h], gr_sem.at[h]).wait()
        for i, ref in enumerate((dk_ref, dv_ref)):
            terms = grecv[h, 0, i].astype(jnp.float32) + grecv[h, 1, i].astype(jnp.float32)
            ref[:, kcol] = (own[h, i] + terms).astype(jnp.bfloat16)
        rest = recvb.at[pl.ds(0, SPLIT - 1), :, wide]
        pltpu.make_async_copy(rest, rest, arecv.at[h]).wait()
        pltpu.make_async_copy(sendb.at[c, :, wide], recvb.at[c, :, wide], aself.at[h]).wait()
        got = recvb[:, :, wide].astype(jnp.float32)
        att_ref[:, wide] = got[:, :SLAB].reshape(ROWS, PER * W).astype(jnp.bfloat16)
        dq_ref[:, wide] = got[:, SLAB:].reshape(ROWS, PER * W).astype(jnp.bfloat16)
        return 0

    lax.fori_loop(0, KV, finish, 0)

    pltpu.make_async_copy(halo, halo, hsend).wait()
    rest = sendb.at[pl.ds(0, SPLIT - 1)]
    pltpu.make_async_copy(rest, rest, asend).wait()
    pltpu.make_async_copy(gsend, gsend, gs_sem).wait()


def on_device(q, k, v, do, doc, plan):
    any_spec = pl.BlockSpec(memory_space=pl.ANY)
    vmem = pl.BlockSpec(memory_space=pltpu.VMEM)
    bf16 = jnp.bfloat16
    return pl.pallas_call(
        kernel,
        out_shape=[
            jax.ShapeDtypeStruct(q.shape, bf16),
            jax.ShapeDtypeStruct(q.shape, bf16),
            jax.ShapeDtypeStruct(k.shape, bf16),
            jax.ShapeDtypeStruct(v.shape, bf16),
        ],
        in_specs=[any_spec] * 6,
        out_specs=[vmem] * 4,
        scratch_shapes=[
            pltpu.VMEM(q.shape, bf16),
            pltpu.VMEM(q.shape, bf16),
            pltpu.VMEM(k.shape, bf16),
            pltpu.VMEM(v.shape, bf16),
            pltpu.SMEM((DOCS,), jnp.int32),
            pltpu.SMEM((SPLIT, SPLIT), jnp.int32),
            pltpu.VMEM((KV, 2, 2 * ROWS, W), bf16),
            pltpu.VMEM((SPLIT, 2 * SLAB, KV * PER * W), bf16),
            pltpu.VMEM((SPLIT, 2 * SLAB, KV * PER * W), bf16),
            pltpu.VMEM((KV, 2, 2, ROWS, W), bf16),
            pltpu.VMEM((KV, 2, 2, ROWS, W), bf16),
            pltpu.VMEM((KV, 2, ROWS, W), jnp.float32),
            pltpu.VMEM((3 * ROWS, ROWS), jnp.float32),
            pltpu.VMEM((2 * ROWS, 2 * ROWS), bf16),
            pltpu.SemaphoreType.DMA((4,)),
            pltpu.SemaphoreType.DMA((2,)),
            pltpu.SemaphoreType.DMA,
            pltpu.SemaphoreType.DMA((KV,)),
            pltpu.SemaphoreType.DMA,
            pltpu.SemaphoreType.DMA((KV,)),
            pltpu.SemaphoreType.DMA((KV,)),
            pltpu.SemaphoreType.DMA,
            pltpu.SemaphoreType.DMA((KV,)),
        ],
        compiler_params=pltpu.CompilerParams(
            collective_id=0, has_side_effects=True, vmem_limit_bytes=60 << 20
        ),
    )(q, do, k, v, doc, plan)


def solution(mesh):
    rows = P(("dp", "ctx"), None)
    return jax.shard_map(
        on_device,
        mesh=mesh,
        in_specs=(rows, rows, rows, rows, P(), P("dp", None, None)),
        out_specs=(rows, rows, rows, rows),
        check_vma=False,
    )
```

time: 374 us -> 59.9 us (0.16)
  waiting for transfers between devices: 190 us -> 0 us
  local copies, waits for them, and re-layouts: 74.8 us -> 5.01 us
  Pallas kernels: 0 us -> 53.5 us
  other arithmetic: 40.9 us -> 0 us
  starting transfers between devices: 26.4 us -> 0 us
  matrix products: 23.1 us -> 0 us
  between operations: 14.6 us -> 0.65 us
    reduce_scatter x2 -> x0, waiting for transfers between devices: 104 us -> none  [the longest x1 78.9 us: on_device(): lax.psum_scatter(own_v, 'ctx', scatter_dimension=0, tiled=True)]
    all_gather x2 -> x0, waiting for transfers between devices: 66.7 us -> none  [the longest x1 41.7 us: on_device(): lax.all_gather(key_matrix, 'ctx', axis=0, tiled=True)]
    pallas_call x0 -> x1, Pallas kernels: none -> 53.5 us  [on_device(): pl.pallas_call(kernel, out_shape=[jax.ShapeDtypeStruct(q.shape, bf16), ja...]
    concatenate x4 -> x0, local copies, waits for them, and re-layouts: 25.6 us -> none  [the longest x1 12.7 us: attend_over_span(): jnp.concatenate(value_terms, axis=1)]
    dot_general x24 -> x0, matrix products: 23.1 us -> none  [the longest x4 5.41 us: attend_over_span(): jnp.einsum('igd,jd->gij', delta_block, value_block_tile, preferred_elemen...]
    concatenate x6 -> x0, other arithmetic: 22.2 us -> none  [the longest x2 9.77 us: cut_windows(): jnp.concatenate([segments[:-2], segments[1:-1], segments[2:]], axis=1)]
    squeeze x2 -> x0, local copies, waits for them, and re-layouts: 20.5 us -> none  [fold_tiles(): total = total + jnp.pad(tiles[:, tile], ((tile, 2 - tile), (0, 0), (0, 0)))]
    all_to_all x2 -> x0, waiting for transfers between devices: 16.4 us -> none  [the longest x1 16.3 us: on_device(): lax.all_to_all(send_q, 'ctx', split_axis=0, concat_axis=0, tiled=True)]
  transfers between devices with their start and end apart: 10 -> 0, of which waited for: 6 -> 0; matrix products, arithmetic and copies ran while one was open for 16% -> 0% of each run, Pallas kernels for 0% -> 0%
where the time goes in v1:
time: 59.9 us; the launch traced here: 59.1 us
  Pallas kernels  53.5 us (89%)
  local copies, waits for them, and re-layouts  5.01 us (8%)
  between operations  0.65 us (1%)
    pallas_call x1, Pallas kernels, on_device(): pl.pallas_call(kernel, out_shape=[jax.ShapeDtypeStruct(q.shape, bf16), ja...  53.5 us
    unnamed x10, local copies, waits for them, and re-layouts  5.01 us

profile of v1, /device:TPU:7, one launch (start us, length us, event | category | flops | bytes accessed | tf_op | source)
XLA Modules:
  0.0 59.1 jit_solution(14090655951124049185)
XLA Ops:
  0.6 53.5 %shard_map.93 = (bf16[128,4096]{1,0:T(8,128)(2,1)}, bf16[128,4096]{1,0:T(8,128)(2,1)}, bf16[128,512]{1,0:T(8,128)(2,1)}, bf16[128,512]{1,0:T(8,128)(2,1)}) custom-call(bf16[128,4096]{1,0:T(8,128)(2,1)} %q_hbm.1, bf16[128,4096]{1,0:T(8,128)(2,1)} %do_hbm.1, bf16[128,512]{1,0:T(8,128)(2,1)} %k_hbm.1, bf16[128,512]{1,0:T(8,128)(2,1)} %v_hbm.1, s32[96]{0:T(128)} %doc_hbm.1, ...), custom_call_target="tpu_custom_call" | custom-call | tf_op jit(solution)/shard_map/pallas_call | solution.py:209
  54.1 0.0 copy-start
  54.1 2.4 %copy.14 = bf16[128,4096]{1,0:T(8,128)(2,1)} copy(bf16[128,4096]{1,0:T(8,128)(2,1)} %get-tuple-element.8) | data formatting | bytes 2097152
  56.5 0.0 copy-done
  56.5 0.0 copy-start.2
  56.5 1.0 %copy.15 = bf16[128,4096]{1,0:T(8,128)(2,1)} copy(bf16[128,4096]{1,0:T(8,128)(2,1)S(1)} %copy-done) | data formatting | bytes 2097152
  57.5 0.1 copy-done.2
  57.5 0.0 copy-start.1
  57.5 0.7 %copy.16 = bf16[128,512]{1,0:T(8,128)(2,1)} copy(bf16[128,512]{1,0:T(8,128)(2,1)S(1)} %copy-done.2) | data formatting | bytes 262144
  58.2 0.3 copy-done.1
  58.5 0.7 %copy.17 = bf16[128,512]{1,0:T(8,128)(2,1)} copy(bf16[128,512]{1,0:T(8,128)(2,1)S(1)} %copy-done.1) | data formatting | bytes 262144
Async XLA Ops:
  54.1 2.4 %copy-start = (bf16[128,4096]{1,0:T(8,128)(2,1)S(1)}, bf16[128,4096]{1,0:T(8,128)(2,1)}, u32[]{:S(2)}) copy-start(bf16[128,4096]{1,0:T(8,128)(2,1)} %get-tuple-element.9) | copy-start | bytes 3145732
  56.5 1.0 %copy-start.2 = (bf16[128,512]{1,0:T(8,128)(2,1)S(1)}, bf16[128,512]{1,0:T(8,128)(2,1)}, u32[]{:S(2)}) copy-start(bf16[128,512]{1,0:T(8,128)(2,1)} %get-tuple-element.10) | copy-start | bytes 393220
  57.5 1.0 %copy-start.1 = (bf16[128,512]{1,0:T(8,128)(2,1)S(1)}, bf16[128,512]{1,0:T(8,128)(2,1)}, u32[]{:S(2)}) copy-start(bf16[128,512]{1,0:T(8,128)(2,1)} %get-tuple-element.11) | copy-start | bytes 393220

commit v2 on v1

--- a/solution.py
+++ b/solution.py
@@ -15,6 +15,7 @@
 SPLIT = 16
 SLAB = ROWS // SPLIT
 GROUPS = 8
+SIDE = 4
 DOCS = 96
 PAIR = 2
 MESH = pl.DeviceIdType.MESH
@@ -35,7 +36,7 @@
     q_hbm, do_hbm, k_hbm, v_hbm, doc_hbm, plan_hbm,
     att_ref, dq_ref, dk_ref, dv_ref,
     q_v, do_v, k_v, v_v, doc_s, plan_s, halo, sendb, recvb, gsend, grecv, own, bias, perm,
-    load_sem, small_sem, hsend, hrecv, asend, arecv, aself, gs_sem, gr_sem,
+    load_sem, small_sem, hsend, hrecv, asend, arecv, aself, gs_sem, gr_sem, known,
 ):
     g, c = lax.axis_index("dp"), lax.axis_index("ctx")
     line = g * SPLIT + c
@@ -45,15 +46,25 @@
         other = (line + by + total) % total
         return (other // SPLIT, other % SPLIT)
 
+    def on_line(by):
+        return (line + by >= 0) & (line + by < total)
+
+    y, z = c // SIDE, c % SIDE
+
+    def at(dy, dz):
+        return (g, (y + dy) % SIDE * SIDE + (z + dz) % SIDE)
+
+    row = [at(0, by) for by in range(1, SIDE)]
+    column = [at(by, 0) for by in range(1, SIDE)]
     barrier = pltpu.get_barrier_semaphore()
     for by in (1, 2, -1, -2):
-        pl.semaphore_signal(barrier, inc=1, device_id=along(by), device_id_type=MESH)
-
-    def greet(k, _):
-        pl.semaphore_signal(barrier, inc=1, device_id=(g, (c + k) % SPLIT), device_id_type=MESH)
-        return 0
-
-    lax.fori_loop(1, SPLIT, greet, 0)
+
+        @pl.when(on_line(by))
+        def _(by=by):
+            pl.semaphore_signal(barrier, inc=1, device_id=along(by), device_id_type=MESH)
+
+    for other in row + column:
+        pl.semaphore_signal(barrier, inc=1, device_id=other, device_id_type=MESH)
 
     loads = [
         pltpu.make_async_copy(src, dst, load_sem.at[i])
@@ -65,6 +76,38 @@
     ]
     for copy in smalls + loads:
         copy.start()
+
+    fill = jnp.zeros((KV, 2, ROWS, W), jnp.bfloat16)
+    for by in (1, 2):
+
+        @pl.when(jnp.logical_not(on_line(-by)))
+        def _(by=by):
+            halo[:, :, (2 - by) * ROWS : (3 - by) * ROWS] = fill
+
+        @pl.when(jnp.logical_not(on_line(by)))
+        def _(by=by):
+            grecv[:, by - 1] = fill
+
+    near = sum(on_line(by).astype(jnp.int32) for by in (1, 2, -1, -2))
+    pl.semaphore_wait(barrier, near + len(row) + len(column))
+
+    for h in range(KV):
+        for by in (1, 2):
+
+            @pl.when(on_line(by))
+            def _(h=h, by=by):
+                for i, src in enumerate((k_hbm, v_hbm)):
+                    pltpu.make_async_remote_copy(
+                        src_ref=src.at[:, pl.ds(h * W, W)],
+                        dst_ref=halo.at[h, i, pl.ds((2 - by) * ROWS, ROWS)],
+                        send_sem=hsend.at[by - 1],
+                        recv_sem=hrecv.at[h, by - 1],
+                        device_id=along(by),
+                        device_id_type=MESH,
+                    ).start()
+
+    for other in row:
+        pl.semaphore_signal(known, inc=1, device_id=other, device_id_type=MESH)
 
     for copy in smalls:
         copy.wait()
@@ -92,24 +135,17 @@
         0.0,
     ).astype(jnp.bfloat16)
 
-    pl.semaphore_wait(barrier, SPLIT - 1 + 4)
-
-    for h in range(KV):
-        for i, src in enumerate((k_hbm, v_hbm)):
-            for by in (1, 2):
-                pltpu.make_async_remote_copy(
-                    src_ref=src.at[:, pl.ds(h * W, W)],
-                    dst_ref=halo.at[h, i, pl.ds((2 - by) * ROWS, ROWS)],
-                    send_sem=hsend,
-                    recv_sem=hrecv.at[h],
-                    device_id=along(by),
-                    device_id_type=MESH,
-                ).start()
     for copy in loads:
         copy.wait()
 
     def one_head(h, _):
-        pltpu.make_async_copy(halo.at[h], halo.at[h], hrecv.at[h]).wait()
+        for by in (1, 2):
+
+            @pl.when(on_line(-by))
+            def _(by=by):
+                part = halo.at[h, :, pl.ds((2 - by) * ROWS, ROWS)]
+                pltpu.make_async_copy(part, part, hrecv.at[h, by - 1]).wait()
+
         kcol = pl.ds(pl.multiple_of(h * W, W), W)
         kw = jnp.concatenate([halo[h, 0], k_v[:, kcol]], axis=0)
         vw = jnp.concatenate([halo[h, 1], v_v[:, kcol]], axis=0)
@@ -144,8 +180,8 @@
                 sendb[:, :, cols[s]] = message.reshape(SPLIT, 2 * SLAB, W)
             span = pl.ds(pl.multiple_of(base, W), PAIR * W)
 
-            def send(k, _, span=span):
-                d = (c + k) % SPLIT
+            def send(dy, dz, span=span):
+                _, d = at(dy, dz)
                 pltpu.make_async_remote_copy(
                     src_ref=sendb.at[d, :, span],
                     dst_ref=recvb.at[c, :, span],
@@ -154,9 +190,21 @@
                     device_id=(g, d),
                     device_id_type=MESH,
                 ).start()
+
+            for by in range(1, SIDE):
+                send(0, by)
+                send(by, 0)
+            if p == 0:
+
+                @pl.when(h == 0)
+                def _():
+                    pl.semaphore_wait(known, SIDE - 1)
+
+            def send_far(k, _, send=send):
+                send(k // (SIDE - 1) + 1, (k + k // (SIDE - 1)) % (SIDE - 1) + 1)
                 return 0
 
-            lax.fori_loop(1, SPLIT, send, 0)
+            lax.fori_loop(0, (SIDE - 1) ** 2, send_far, 0)
         dk = dk * SCALE
         own[h, 0] = dk[2 * ROWS :]
         own[h, 1] = dv[2 * ROWS :]
@@ -165,14 +213,18 @@
         gsend[h, 1, 0] = dk[:ROWS].astype(jnp.bfloat16)
         gsend[h, 1, 1] = dv[:ROWS].astype(jnp.bfloat16)
         for by in (1, 2):
-            pltpu.make_async_remote_copy(
-                src_ref=gsend.at[h, by - 1],
-                dst_ref=grecv.at[h, by - 1],
-                send_sem=gs_sem,
-                recv_sem=gr_sem.at[h],
-                device_id=along(-by),
-                device_id_type=MESH,
-            ).start()
+
+            @pl.when(on_line(-by))
+            def _(by=by):
+                pltpu.make_async_remote_copy(
+                    src_ref=gsend.at[h, by - 1],
+                    dst_ref=grecv.at[h, by - 1],
+                    send_sem=gs_sem.at[by - 1],
+                    recv_sem=gr_sem.at[h, by - 1],
+                    device_id=along(-by),
+                    device_id_type=MESH,
+                ).start()
+
         wide = pl.ds(pl.multiple_of(h * PER * W, W), PER * W)
         pltpu.make_async_copy(sendb.at[c, :, wide], recvb.at[c, :, wide], aself.at[h]).start()
         return 0
@@ -182,7 +234,13 @@
     def finish(h, _):
         kcol = pl.ds(pl.multiple_of(h * W, W), W)
         wide = pl.ds(pl.multiple_of(h * PER * W, W), PER * W)
-        pltpu.make_async_copy(grecv.at[h], grecv.at[h], gr_sem.at[h]).wait()
+        for by in (1, 2):
+
+            @pl.when(on_line(by))
+            def _(by=by):
+                part = grecv.at[h, by - 1]
+                pltpu.make_async_copy(part, part, gr_sem.at[h, by - 1]).wait()
+
         for i, ref in enumerate((dk_ref, dv_ref)):
             terms = grecv[h, 0, i].astype(jnp.float32) + grecv[h, 1, i].astype(jnp.float32)
             ref[:, kcol] = (own[h, i] + terms).astype(jnp.bfloat16)
@@ -196,24 +254,43 @@
 
     lax.fori_loop(0, KV, finish, 0)
 
-    pltpu.make_async_copy(halo, halo, hsend).wait()
+    for by in (1, 2):
+
+        @pl.when(on_line(by))
+        def _(by=by):
+            part = halo.at[:, :, pl.ds(0, ROWS)]
+            pltpu.make_async_copy(part, part, hsend.at[by - 1]).wait()
+
+        @pl.when(on_line(-by))
+        def _(by=by):
+            part = gsend.at[:, by - 1]
+            pltpu.make_async_copy(part, part, gs_sem.at[by - 1]).wait()
+
     rest = sendb.at[pl.ds(0, SPLIT - 1)]
     pltpu.make_async_copy(rest, rest, asend).wait()
-    pltpu.make_async_copy(gsend, gsend, gs_sem).wait()
+
+
+def write_out(a_in, b_in, c_in, d_in, a_out, b_out, c_out, d_out, sems):
+    copies = [
+        pltpu.make_async_copy(src, dst, sems.at[i])
+        for i, (src, dst) in enumerate(((a_in, a_out), (b_in, b_out), (c_in, c_out), (d_in, d_out)))
+    ]
+    for copy in copies:
+        copy.start()
+    for copy in copies:
+        copy.wait()
 
 
 def on_device(q, k, v, do, doc, plan):
+    q, k, v, do, doc, plan = (
+        pltpu.with_memory_space_constraint(x, pltpu.HBM) for x in (q, k, v, do, doc, plan)
+    )
     any_spec = pl.BlockSpec(memory_space=pl.ANY)
     vmem = pl.BlockSpec(memory_space=pltpu.VMEM)
     bf16 = jnp.bfloat16
-    return pl.pallas_call(
+    parts = pl.pallas_call(
         kernel,
-        out_shape=[
-            jax.ShapeDtypeStruct(q.shape, bf16),
-            jax.ShapeDtypeStruct(q.shape, bf16),
-            jax.ShapeDtypeStruct(k.shape, bf16),
-            jax.ShapeDtypeStruct(v.shape, bf16),
-        ],
+        out_shape=[pltpu.VMEM(x.shape, bf16) for x in (q, q, k, v)],
         in_specs=[any_spec] * 6,
         out_specs=[vmem] * 4,
         scratch_shapes=[
@@ -233,18 +310,26 @@
             pltpu.VMEM((2 * ROWS, 2 * ROWS), bf16),
             pltpu.SemaphoreType.DMA((4,)),
             pltpu.SemaphoreType.DMA((2,)),
-            pltpu.SemaphoreType.DMA,
-            pltpu.SemaphoreType.DMA((KV,)),
+            pltpu.SemaphoreType.DMA((2,)),
+            pltpu.SemaphoreType.DMA((KV, 2)),
             pltpu.SemaphoreType.DMA,
             pltpu.SemaphoreType.DMA((KV,)),
             pltpu.SemaphoreType.DMA((KV,)),
-            pltpu.SemaphoreType.DMA,
-            pltpu.SemaphoreType.DMA((KV,)),
+            pltpu.SemaphoreType.DMA((2,)),
+            pltpu.SemaphoreType.DMA((KV, 2)),
+            pltpu.SemaphoreType.REGULAR,
         ],
         compiler_params=pltpu.CompilerParams(
-            collective_id=0, has_side_effects=True, vmem_limit_bytes=60 << 20
+            collective_id=0, has_side_effects=True, vmem_limit_bytes=32 << 20
         ),
     )(q, do, k, v, doc, plan)
+    return pl.pallas_call(
+        write_out,
+        out_shape=[jax.ShapeDtypeStruct(x.shape, bf16) for x in (q, q, k, v)],
+        in_specs=[any_spec] * 4,
+        out_specs=[any_spec] * 4,
+        scratch_shapes=[pltpu.SemaphoreType.DMA((4,))],
+    )(*(pltpu.with_memory_space_constraint(x, pltpu.VMEM) for x in parts))
 
 
 def solution(mesh):

time: 59.9 us -> 53.7 us (0.90); the launches traced: 59.1 us -> 53.6 us
  local copies, waits for them, and re-layouts: 5.01 us -> 0 us
    unnamed x10 -> x0, local copies, waits for them, and re-layouts: 5.01 us -> none
    pallas_call x1 -> x2, Pallas kernels: 53.5 us -> 53 us  [the longest x1 51.6 us: on_device(): pl.pallas_call(kernel, out_shape=[pltpu.VMEM(x.shape, bf16) for x in (q,...]
where the time goes in v2:
time: 53.7 us; the launch traced here: 53.6 us
  Pallas kernels  53 us (99%)
  between operations  0.64 us (1%)
    pallas_call x1, Pallas kernels, on_device(): pl.pallas_call(kernel, out_shape=[pltpu.VMEM(x.shape, bf16) for x in (q,...  51.6 us
    pallas_call x1, Pallas kernels, on_device(): pl.pallas_call(write_out, out_shape=[jax.ShapeDtypeStruct(x.shape, bf16)...  1.43 us

profile of v2, /device:TPU:7, one launch (start us, length us, event | category | flops | bytes accessed | tf_op | source)
XLA Modules:
  0.0 53.6 jit_solution(1199881339211332283)
XLA Ops:
  0.6 51.6 %shard_map.93 = (bf16[128,4096]{1,0:T(8,128)(2,1)S(1)}, bf16[128,4096]{1,0:T(8,128)(2,1)S(1)}, bf16[128,512]{1,0:T(8,128)(2,1)S(1)}, bf16[128,512]{1,0:T(8,128)(2,1)S(1)}) custom-call(bf16[128,4096]{1,0:T(8,128)(2,1)} %q_hbm.1, bf16[128,4096]{1,0:T(8,128)(2,1)} %do_hbm.1, bf16[128,512]{1,0:T(8,128)(2,1)} %k_hbm.1, bf16[128,512]{1,0:T(8,128)(2,1)} %v_hbm.1, ...), custom_call_target="tpu_custom_call" | custom-call | tf_op jit(solution)/shard_map/pallas_call | solution.py:291
  52.2 1.4 %shard_map.94 = (bf16[128,4096]{1,0:T(8,128)(2,1)}, bf16[128,4096]{1,0:T(8,128)(2,1)}, bf16[128,512]{1,0:T(8,128)(2,1)}, bf16[128,512]{1,0:T(8,128)(2,1)}) custom-call(bf16[128,4096]{1,0:T(8,128)(2,1)S(1)} %get-tuple-element.8.a_in, bf16[128,4096]{1,0:T(8,128)(2,1)S(1)} %get-tuple-element.9.b_in, bf16[128,512]{1,0:T(8,128)(2,1)S(1)} %get-tuple-element.10.c_in, ...), custom_call_target="tpu_custom_call" | custom-call | tf_op jit(solution)/shard_map/pallas_call | solution.py:326

commit v3 on v2

--- a/solution.py
+++ b/solution.py
@@ -18,6 +18,7 @@
 SIDE = 4
 DOCS = 96
 PAIR = 2
+RELAYED = 1
 MESH = pl.DeviceIdType.MESH
 NT = (((1,), (1,)), ((), ()))
 SCALE = 1.0 / math.sqrt(W)
@@ -35,8 +36,8 @@
 def kernel(
     q_hbm, do_hbm, k_hbm, v_hbm, doc_hbm, plan_hbm,
     att_ref, dq_ref, dk_ref, dv_ref,
-    q_v, do_v, k_v, v_v, doc_s, plan_s, halo, sendb, recvb, gsend, grecv, own, bias, perm,
-    load_sem, small_sem, hsend, hrecv, asend, arecv, aself, gs_sem, gr_sem, known,
+    q_v, do_v, k_v, v_v, doc_s, plan_s, halo, sendb, recvb, gsend, grecv, relay, own, bias, perm,
+    load_sem, small_sem, hsend, hrecv, asend, arecv, aself, gs_sem, gr_sem, relay_recv, relay_send, known,
 ):
     g, c = lax.axis_index("dp"), lax.axis_index("ctx")
     line = g * SPLIT + c
@@ -45,6 +46,9 @@
     def along(by):
         other = (line + by + total) % total
         return (other // SPLIT, other % SPLIT)
+
+    odd = line % 2 == 1
+    even = line % 2 == 0
 
     def on_line(by):
         return (line + by >= 0) & (line + by < total)
@@ -92,7 +96,7 @@
     pl.semaphore_wait(barrier, near + len(row) + len(column))
 
     for h in range(KV):
-        for by in (1, 2):
+        for by in (2, 1):
 
             @pl.when(on_line(by))
             def _(h=h, by=by):
@@ -212,24 +216,52 @@
         gsend[h, 0, 1] = dv[ROWS : 2 * ROWS].astype(jnp.bfloat16)
         gsend[h, 1, 0] = dk[:ROWS].astype(jnp.bfloat16)
         gsend[h, 1, 1] = dv[:ROWS].astype(jnp.bfloat16)
-        for by in (1, 2):
-
-            @pl.when(on_line(-by))
-            def _(by=by):
-                pltpu.make_async_remote_copy(
-                    src_ref=gsend.at[h, by - 1],
-                    dst_ref=grecv.at[h, by - 1],
-                    send_sem=gs_sem.at[by - 1],
-                    recv_sem=gr_sem.at[h, by - 1],
-                    device_id=along(-by),
-                    device_id_type=MESH,
-                ).start()
+        def give(by, dst, sem, other):
+            pltpu.make_async_remote_copy(
+                src_ref=gsend.at[h, by - 1],
+                dst_ref=dst,
+                send_sem=gs_sem.at[by - 1],
+                recv_sem=sem,
+                device_id=other,
+                device_id_type=MESH,
+            ).start()
+
+        @pl.when(on_line(-1))
+        def _():
+            give(1, grecv.at[h, 0], gr_sem.at[h, 0], along(-1))
+
+        around = odd & (h < RELAYED) & ((z != 1) | (y != 0))
+
+        @pl.when(on_line(-2) & jnp.logical_not(around))
+        def _():
+            give(2, grecv.at[h, 1], gr_sem.at[h, 1], along(-2))
+
+        @pl.when(on_line(-2) & around)
+        def _():
+            give(2, relay.at[h], relay_recv.at[h], at(0, 1))
 
         wide = pl.ds(pl.multiple_of(h * PER * W, W), PER * W)
         pltpu.make_async_copy(sendb.at[c, :, wide], recvb.at[c, :, wide], aself.at[h]).start()
         return 0
 
     lax.fori_loop(0, KV, one_head, 0)
+
+    below = line - z + (z + SIDE - 1) % SIDE
+    carries = even & (below >= 2) & ((z != 2) | (y != 0))
+
+    @pl.when(carries)
+    def _():
+        for h in range(RELAYED):
+            pltpu.make_async_copy(relay.at[h], relay.at[h], relay_recv.at[h]).wait()
+            pltpu.make_async_remote_copy(
+                src_ref=relay.at[h],
+                dst_ref=grecv.at[h, 1],
+                send_sem=relay_send,
+                recv_sem=gr_sem.at[h, 1],
+                device_id=((below - 2) // SPLIT, (below - 2) % SPLIT),
+                device_id_type=MESH,
+            ).start()
+
 
     def finish(h, _):
         kcol = pl.ds(pl.multiple_of(h * W, W), W)
@@ -268,6 +300,10 @@
 
     rest = sendb.at[pl.ds(0, SPLIT - 1)]
     pltpu.make_async_copy(rest, rest, asend).wait()
+
+    @pl.when(carries)
+    def _():
+        pltpu.make_async_copy(relay, relay, relay_send).wait()
 
 
 def write_out(a_in, b_in, c_in, d_in, a_out, b_out, c_out, d_out, sems):
@@ -305,6 +341,7 @@
             pltpu.VMEM((SPLIT, 2 * SLAB, KV * PER * W), bf16),
             pltpu.VMEM((KV, 2, 2, ROWS, W), bf16),
             pltpu.VMEM((KV, 2, 2, ROWS, W), bf16),
+            pltpu.VMEM((RELAYED, 2, ROWS, W), bf16),
             pltpu.VMEM((KV, 2, ROWS, W), jnp.float32),
             pltpu.VMEM((3 * ROWS, ROWS), jnp.float32),
             pltpu.VMEM((2 * ROWS, 2 * ROWS), bf16),
@@ -317,6 +354,8 @@
             pltpu.SemaphoreType.DMA((KV,)),
             pltpu.SemaphoreType.DMA((2,)),
             pltpu.SemaphoreType.DMA((KV, 2)),
+            pltpu.SemaphoreType.DMA((RELAYED,)),
+            pltpu.SemaphoreType.DMA,
             pltpu.SemaphoreType.REGULAR,
         ],
         compiler_params=pltpu.CompilerParams(

time: 53.7 us -> 52.6 us (0.980)
  Pallas kernels: 53 us -> 51.9 us
    pallas_call x1, Pallas kernels: 51.6 us -> 50.4 us  [on_device(): pl.pallas_call(kernel, out_shape=[pltpu.VMEM(x.shape, bf16) for x in (q,...]
where the time goes in v3:
time: 52.6 us; the launch traced here: 52.5 us
  Pallas kernels  51.9 us (99%)
  between operations  0.64 us (1%)
    pallas_call x1, Pallas kernels, on_device(): pl.pallas_call(kernel, out_shape=[pltpu.VMEM(x.shape, bf16) for x in (q,...  50.4 us
    pallas_call x1, Pallas kernels, on_device(): pl.pallas_call(write_out, out_shape=[jax.ShapeDtypeStruct(x.shape, bf16)...  1.43 us

profile of v3, /device:TPU:7, one launch (start us, length us, event | category | flops | bytes accessed | tf_op | source)
XLA Modules:
  0.0 52.5 jit_solution(1206569546173869688)
XLA Ops:
  0.6 50.4 %shard_map.93 = (bf16[128,4096]{1,0:T(8,128)(2,1)S(1)}, bf16[128,4096]{1,0:T(8,128)(2,1)S(1)}, bf16[128,512]{1,0:T(8,128)(2,1)S(1)}, bf16[128,512]{1,0:T(8,128)(2,1)S(1)}) custom-call(bf16[128,4096]{1,0:T(8,128)(2,1)} %q_hbm.1, bf16[128,4096]{1,0:T(8,128)(2,1)} %do_hbm.1, bf16[128,512]{1,0:T(8,128)(2,1)} %k_hbm.1, bf16[128,512]{1,0:T(8,128)(2,1)} %v_hbm.1, ...), custom_call_target="tpu_custom_call" | custom-call | tf_op jit(solution)/shard_map/pallas_call | solution.py:327
  51.1 1.4 %shard_map.94 = (bf16[128,4096]{1,0:T(8,128)(2,1)}, bf16[128,4096]{1,0:T(8,128)(2,1)}, bf16[128,512]{1,0:T(8,128)(2,1)}, bf16[128,512]{1,0:T(8,128)(2,1)}) custom-call(bf16[128,4096]{1,0:T(8,128)(2,1)S(1)} %get-tuple-element.8.a_in, bf16[128,4096]{1,0:T(8,128)(2,1)S(1)} %get-tuple-element.9.b_in, bf16[128,512]{1,0:T(8,128)(2,1)S(1)} %get-tuple-element.10.c_in, ...), custom_call_target="tpu_custom_call" | custom-call | tf_op jit(solution)/shard_map/pallas_call | solution.py:365

commit v4 on v3

--- a/solution.py
+++ b/solution.py
@@ -95,8 +95,9 @@
     near = sum(on_line(by).astype(jnp.int32) for by in (1, 2, -1, -2))
     pl.semaphore_wait(barrier, near + len(row) + len(column))
 
-    for h in range(KV):
-        for by in (2, 1):
+    far_first = [(0, 2), (0, 1)] + [(h, by) for by in (2, 1) for h in range(1, KV)]
+    for h, by in far_first:
+        if True:
 
             @pl.when(on_line(by))
             def _(h=h, by=by):
@@ -195,9 +196,22 @@
                     device_id_type=MESH,
                 ).start()
 
-            for by in range(1, SIDE):
-                send(0, by)
-                send(by, 0)
+            @pl.when(h == KV - 1)
+            def _(send=send):
+                for far in range(2 * SIDE - 1):
+                    for ty in range(SIDE):
+                        if 0 <= far - ty < SIDE:
+
+                            @pl.when(c != ty * SIDE + far - ty)
+                            def _(ty=ty, tz=far - ty):
+                                send(ty - y + SIDE, tz - z + SIDE)
+
+            @pl.when(h < KV - 1)
+            def _(send=send):
+                for by in range(1, SIDE):
+                    send(0, by)
+                    send(by, 0)
+
             if p == 0:
 
                 @pl.when(h == 0)
@@ -208,7 +222,10 @@
                 send(k // (SIDE - 1) + 1, (k + k // (SIDE - 1)) % (SIDE - 1) + 1)
                 return 0
 
-            lax.fori_loop(0, (SIDE - 1) ** 2, send_far, 0)
+            @pl.when(h < KV - 1)
+            def _(send_far=send_far):
+                lax.fori_loop(0, (SIDE - 1) ** 2, send_far, 0)
+
         dk = dk * SCALE
         own[h, 0] = dk[2 * ROWS :]
         own[h, 1] = dv[2 * ROWS :]

time: 52.6 us -> 52.6 us (level)
  no operation moved by 1% of the time
where the time goes in v4:
time: 52.6 us; the launch traced here: 52.5 us
  Pallas kernels  51.9 us (99%)
  between operations  0.64 us (1%)
    pallas_call x1, Pallas kernels, on_device(): pl.pallas_call(kernel, out_shape=[pltpu.VMEM(x.shape, bf16) for x in (q,...  50.4 us
    pallas_call x1, Pallas kernels, on_device(): pl.pallas_call(write_out, out_shape=[jax.ShapeDtypeStruct(x.shape, bf16)...  1.43 us

profile of v4, /device:TPU:7, one launch (start us, length us, event | category | flops | bytes accessed | tf_op | source)
XLA Modules:
  0.0 52.5 jit_solution(10681144590962643917)
XLA Ops:
  0.6 50.4 %shard_map.93 = (bf16[128,4096]{1,0:T(8,128)(2,1)S(1)}, bf16[128,4096]{1,0:T(8,128)(2,1)S(1)}, bf16[128,512]{1,0:T(8,128)(2,1)S(1)}, bf16[128,512]{1,0:T(8,128)(2,1)S(1)}) custom-call(bf16[128,4096]{1,0:T(8,128)(2,1)} %q_hbm.1, bf16[128,4096]{1,0:T(8,128)(2,1)} %do_hbm.1, bf16[128,512]{1,0:T(8,128)(2,1)} %k_hbm.1, bf16[128,512]{1,0:T(8,128)(2,1)} %v_hbm.1, ...), custom_call_target="tpu_custom_call" | custom-call | tf_op jit(solution)/shard_map/pallas_call | solution.py:344
  51.1 1.4 %shard_map.94 = (bf16[128,4096]{1,0:T(8,128)(2,1)}, bf16[128,4096]{1,0:T(8,128)(2,1)}, bf16[128,512]{1,0:T(8,128)(2,1)}, bf16[128,512]{1,0:T(8,128)(2,1)}) custom-call(bf16[128,4096]{1,0:T(8,128)(2,1)S(1)} %get-tuple-element.8.a_in, bf16[128,4096]{1,0:T(8,128)(2,1)S(1)} %get-tuple-element.9.b_in, bf16[128,512]{1,0:T(8,128)(2,1)S(1)} %get-tuple-element.10.c_in, ...), custom_call_target="tpu_custom_call" | custom-call | tf_op jit(solution)/shard_map/pallas_call | solution.py:382
